TPU v7x, 32 devices: a whole 2x2x4 slice. The times are simulated.
32 devices in a mesh: dp: 2 (over x), row: 4 (over z), col: 4 (over y, core).
Axes of the slice: x: 2, y: 2, z: 4, core: 2. Of those that a mesh axis runs over, the one named last changes fastest.
Arguments:
- inputs: bfloat16 [2304, 4, 384], P(('dp', 'col'), 'row'), may hold values from -6 to 6
- cotangent: bfloat16 [2304, 4, 384], P(('dp', 'col'), 'row'), may hold values from -6 to 6
- slot_mask: int32 [8], replicated, may hold values from 0 to 1, as said below
- region_ids: int32 [24, 24], replicated, may hold values from 0 to 8, as said below
- offset_index: int32 [144, 144], replicated, may hold values from 0 to 528, as said below
- first_gain: float32 [768], P('row'), may hold values from 0.5 to 1.5
- first_shift: float32 [768], P('row'), may hold values from -1.75 to 1.75
- query_key_value: bfloat16 [384, 3, 4, 384], P('row', None, 'col'), may hold values from -0.21875 to 0.21875
- query_value_bias: float32 [2, 768], P(None, 'col'), may hold values from -3 to 3
- position_table: float32 [529, 24], P(None, 'col'), may hold values from -6 to 6
- output_weight: bfloat16 [384, 4, 384], P('col', 'row'), may hold values from -0.625 to 0.625
- output_bias: float32 [768], P('row'), may hold values from -1.75 to 1.75
- second_gain: float32 [768], P('row'), may hold values from 0.5 to 1.5
- second_shift: float32 [768], P('row'), may hold values from -1.75 to 1.75
- expand_weight: bfloat16 [768, 3072], P('row', 'col'), may hold values from -0.21875 to 0.21875
- expand_bias: float32 [3072], P('col'), may hold values from -1.75 to 1.75
- contract_weight: bfloat16 [1536, 4, 384], P('col', 'row'), may hold values from -0.109375 to 0.109375
- contract_bias: float32 [768], P('row'), may hold values from -1.75 to 1.75
Outputs:
- layer_output: bfloat16 [2304, 4, 384], P(('dp', 'col'), 'row')
- input_gradient: float32 [2304, 4, 384], P(('dp', 'col'), 'row')
- first_gain_gradient: float32 [768], P('row')
- first_shift_gradient: float32 [768], P('row')
- query_key_value_gradient: float32 [384, 3, 4, 384], P('row', None, 'col')
- query_value_bias_gradient: float32 [2, 768], P(None, 'col')
- position_table_gradient: float32 [529, 24], P(None, 'col')
- output_weight_gradient: float32 [384, 4, 384], P('col', 'row')
- output_bias_gradient: float32 [768], P('row')
- second_gain_gradient: float32 [768], P('row')
- second_shift_gradient: float32 [768], P('row')
- expand_weight_gradient: float32 [768, 3072], P('row', 'col')
- expand_bias_gradient: float32 [3072], P('col')
- contract_weight_gradient: float32 [1536, 4, 384], P('col', 'row')
- contract_bias_gradient: float32 [768], P('row')
Inputs may be any that keep to these rules, and one draw needn't show every extreme that they name: `slot_mask`: 1 on the first slots and 0 on the rest; at least one slot of each kind. `region_ids`: 3 times a band of the token's row plus a band of its column; bands 0, 1, 2 cut at two drawn places along each side, each band non-empty. `offset_index`: a one-to-one relabelling of the offset between two window positions: equal offsets give equal entries, and every entry appears.
All inputs are finite; a program needn't handle non-finite values.
Results may differ from a plain program's by a relative error of at most 0.012.
Values may be sent and summed in bfloat16 or wider, within the bound.
No kernel may reach another device: no remote copies, remote signals or barrier semaphores. Data moves between devices by JAX's collectives and lax.ppermute only.
A program may use at most 128 MiB of HBM per device.

v0:
```python
import jax
import jax.numpy as jnp
from jax import lax
from jax.sharding import PartitionSpec as P

HEAD_DIM = 32
SIDE = 24
WIN = 12
SHIFT = 6
REL = 529
NORM_EPS = 1e-05
MASK_FILL = -100.0
SPLIT_DIMS = (((1,), (1,)), ((), ()))
ROW_DIMS = (((0,), (0,)), ((), ()))


def unpair_local(paired):
    return paired.reshape(paired.shape[0] * 2, paired.shape[2] // 2)


def pair_local(matrix):
    return matrix.reshape(matrix.shape[0] // 2, 1, matrix.shape[1] * 2)


def unpair_joined(paired):
    halves = paired.shape[0]
    single = paired.shape[3] // 2
    return paired.reshape(halves, 3, 2, single).transpose(0, 2, 1, 3).reshape(halves * 2, 3, single)


def pair_joined(joined):
    count = joined.shape[0]
    single = joined.shape[2]
    return (
        joined.reshape(count // 2, 2, 3, single)
        .transpose(0, 2, 1, 3)
        .reshape(count // 2, 3, 1, 2 * single)
    )


def to_windows(source, head_count):
    images = source.shape[0] // (SIDE * SIDE)
    blocks = SIDE // WIN
    shaped = source.reshape(images, SIDE, SIDE, head_count, HEAD_DIM)
    shaped = jnp.roll(shaped, (-SHIFT, -SHIFT), axis=(1, 2))
    shaped = shaped.reshape(images, blocks, WIN, blocks, WIN, head_count, HEAD_DIM)
    shaped = shaped.transpose(0, 1, 3, 5, 2, 4, 6)
    return shaped.reshape(images * blocks * blocks, head_count, WIN * WIN, HEAD_DIM)


def from_windows(windowed, head_count):
    blocks = SIDE // WIN
    images = windowed.shape[0] // (blocks * blocks)
    shaped = windowed.reshape(images, blocks, blocks, head_count, WIN, WIN, HEAD_DIM)
    shaped = shaped.transpose(0, 1, 4, 2, 5, 3, 6).reshape(images, SIDE, SIDE, head_count, HEAD_DIM)
    shaped = jnp.roll(shaped, (SHIFT, SHIFT), axis=(1, 2))
    return shaped.reshape(images * SIDE * SIDE, head_count * HEAD_DIM)


def region_mask(region_ids):
    blocks = SIDE // WIN
    labels = (
        region_ids.reshape(blocks, WIN, blocks, WIN)
        .transpose(0, 2, 1, 3)
        .reshape(blocks * blocks, WIN * WIN)
    )
    return jnp.where(labels[:, :, None] == labels[:, None, :], 0.0, MASK_FILL).astype(jnp.float32)


def norm_totals(first_term, second_term):
    return lax.psum((jnp.sum(first_term, -1), jnp.sum(second_term, -1)), "row")


def norm_forward(values, norm_gain, norm_shift, width):
    totals, squares = norm_totals(values, values * values)
    centre = totals / width
    spread = squares / width - centre * centre
    inverse = lax.rsqrt(spread + NORM_EPS)
    normed = (values - centre[:, None]) * inverse[:, None]
    return (normed, inverse, normed * norm_gain + norm_shift)


def norm_backward(upstream, normed, inverse, norm_gain, width):
    scaled = upstream * norm_gain
    totals, crossed = norm_totals(scaled, scaled * normed)
    return inverse[:, None] * (
        scaled - totals[:, None] / width - normed * (crossed[:, None] / width)
    )


def norm_spread(values):
    return lax.all_gather(values, "col", axis=0, tiled=True)


def head_collect(values):
    return lax.all_gather(values, "row", axis=0, tiled=True)


def cotangent_spread(values):
    return lax.all_gather(values, "col", axis=0, tiled=True)


def gradient_collect(values):
    return lax.all_gather(values, "row", axis=0, tiled=True)


def width_sums(gathered, weight, row_count):

    def partial_rows(begin_at, how_many):
        return jnp.dot(gathered, weight, preferred_element_type=jnp.float32)

    return lax.psum_scatter(
        partial_rows(jnp.int32(0), lax.axis_size("row") * row_count),
        "row",
        scatter_dimension=0,
        tiled=True,
    )


def token_sums(gathered, weight, row_count):

    def partial_rows(begin_at, how_many):
        return jnp.dot(gathered, weight, preferred_element_type=jnp.float32)

    return lax.psum_scatter(
        partial_rows(jnp.int32(0), lax.axis_size("col") * row_count),
        "col",
        scatter_dimension=0,
        tiled=True,
    )


def width_back(gathered, weight, row_count):

    def partial_rows(begin_at, how_many):
        return lax.dot_general(gathered, weight, SPLIT_DIMS, preferred_element_type=jnp.float32)

    return lax.psum_scatter(
        partial_rows(jnp.int32(0), lax.axis_size("row") * row_count),
        "row",
        scatter_dimension=0,
        tiled=True,
    )


def token_back(gathered, weight, row_count):

    def partial_rows(begin_at, how_many):
        return lax.dot_general(gathered, weight, SPLIT_DIMS, preferred_element_type=jnp.float32)

    return lax.psum_scatter(
        partial_rows(jnp.int32(0), lax.axis_size("col") * row_count),
        "col",
        scatter_dimension=0,
        tiled=True,
    )


def exact_gelu(values):
    return jax.nn.gelu(values, approximate=False)


def gelu_backward(pre_values, upstream):
    return jax.vjp(exact_gelu, pre_values)[1](upstream)[0]


def window_scores(queries, keys_in, bias_block, mask_block):
    products = jnp.einsum("nhid,nhjd->nhij", queries, keys_in, preferred_element_type=jnp.float32)
    return products + bias_block[None] + mask_block[:, None]


def local(
    inputs,
    cotangent,
    slot_mask,
    region_ids,
    offset_index,
    first_gain,
    first_shift,
    query_key_value,
    query_value_bias,
    position_table,
    output_weight,
    output_bias,
    second_gain,
    second_shift,
    expand_weight,
    expand_bias,
    contract_weight,
    contract_bias,
):
    inputs_rows = unpair_local(inputs)
    cotangent_rows = unpair_local(cotangent)
    joined_plain = unpair_joined(query_key_value)
    output_plain = unpair_local(output_weight)
    contract_plain = unpair_local(contract_weight)
    row_size = lax.axis_size("row")
    local_tokens = inputs_rows.shape[0]
    image_tokens = SIDE * SIDE
    width = inputs_rows.shape[1] * row_size
    head_width = joined_plain.shape[2]
    head_local = head_width // HEAD_DIM
    scale = float(HEAD_DIM) ** (-0.5)
    joined_weight = joined_plain.reshape(joined_plain.shape[0], 3 * head_width)
    mask_block = region_mask(region_ids)
    bias_block = jnp.take(position_table, offset_index, axis=0).transpose(2, 0, 1)
    residual = inputs_rows.astype(jnp.float32)
    normed_one, inverse_one, scaled_one = norm_forward(residual, first_gain, first_shift, width)
    spread_one = norm_spread(scaled_one.astype(jnp.bfloat16))
    projected = width_sums(spread_one, joined_weight, image_tokens).reshape(
        image_tokens, 3, head_width
    )
    queries = to_windows(
        ((projected[:, 0] + query_value_bias[0]) * scale).astype(jnp.bfloat16), head_local
    )
    keys_win = to_windows(projected[:, 1].astype(jnp.bfloat16), head_local)
    values_win = to_windows(
        (projected[:, 2] + query_value_bias[1]).astype(jnp.bfloat16), head_local
    )
    scores = window_scores(queries, keys_win, bias_block, mask_block)
    largest = jnp.max(scores, -1, keepdims=True)
    powers = jnp.exp(scores - largest)
    summed = jnp.sum(powers, -1, keepdims=True)
    log_total = largest + jnp.log(summed)
    attended = jnp.einsum(
        "nhij,nhjd->nhid",
        (powers / summed).astype(jnp.bfloat16),
        values_win,
        preferred_element_type=jnp.float32,
    )
    attended_all = head_collect(from_windows(attended.astype(jnp.bfloat16), head_local))
    residual_mid = residual + token_sums(attended_all, output_plain, local_tokens) + output_bias
    normed_two, inverse_two, scaled_two = norm_forward(
        residual_mid, second_gain, second_shift, width
    )
    spread_two = norm_spread(scaled_two.astype(jnp.bfloat16))
    pre_values = width_sums(spread_two, expand_weight, image_tokens) + expand_bias
    hidden_all = head_collect(exact_gelu(pre_values).astype(jnp.bfloat16))
    layer_output = (
        residual_mid + token_sums(hidden_all, contract_plain, local_tokens) + contract_bias
    ).astype(jnp.bfloat16)
    flags = lax.dynamic_slice_in_dim(slot_mask, lax.axis_index("dp") * row_size, row_size)
    positions = lax.axis_index("col") * local_tokens + jnp.arange(local_tokens, dtype=jnp.int32)
    image_slot = positions // image_tokens
    token_flag = jnp.sum(
        jnp.where(
            image_slot[:, None] == jnp.arange(row_size, dtype=jnp.int32)[None, :], flags[None, :], 0
        ),
        axis=1,
    ).astype(jnp.float32)
    upstream = cotangent_rows.astype(jnp.float32) * token_flag[:, None]
    upstream_all = cotangent_spread(upstream.astype(jnp.bfloat16))
    contract_grad = lax.dot_general(
        hidden_all, upstream_all, ROW_DIMS, preferred_element_type=jnp.float32
    )
    contract_bias_grad = jnp.sum(upstream_all, 0, dtype=jnp.float32)
    hidden_grad = width_back(upstream_all, contract_plain, image_tokens)
    pre_grad_all = gradient_collect(gelu_backward(pre_values, hidden_grad).astype(jnp.bfloat16))
    expand_grad = lax.dot_general(
        spread_two, pre_grad_all, ROW_DIMS, preferred_element_type=jnp.float32
    )
    expand_bias_grad = jnp.sum(pre_grad_all, 0, dtype=jnp.float32)
    normed_grad_two = token_back(pre_grad_all, expand_weight, local_tokens)
    second_gain_grad = jnp.sum(normed_grad_two * normed_two, 0)
    second_shift_grad = jnp.sum(normed_grad_two, 0)
    residual_grad = upstream + norm_backward(
        normed_grad_two, normed_two, inverse_two, second_gain, width
    )
    residual_all = cotangent_spread(residual_grad.astype(jnp.bfloat16))
    output_grad = lax.dot_general(
        attended_all, residual_all, ROW_DIMS, preferred_element_type=jnp.float32
    )
    output_bias_grad = jnp.sum(residual_all, 0, dtype=jnp.float32)
    attended_grad = to_windows(
        width_back(residual_all, output_plain, image_tokens).astype(jnp.bfloat16), head_local
    )
    probs = jnp.exp(window_scores(queries, keys_win, bias_block, mask_block) - log_total)
    value_grad = jnp.einsum(
        "nhij,nhid->nhjd",
        probs.astype(jnp.bfloat16),
        attended_grad,
        preferred_element_type=jnp.float32,
    )
    prob_grad = jnp.einsum(
        "nhid,nhjd->nhij", attended_grad, values_win, preferred_element_type=jnp.float32
    )
    score_grad = (probs * (prob_grad - jnp.sum(probs * prob_grad, -1, keepdims=True))).astype(
        jnp.bfloat16
    )
    query_grad = jnp.einsum(
        "nhij,nhjd->nhid", score_grad, keys_win, preferred_element_type=jnp.float32
    )
    key_grad = jnp.einsum(
        "nhij,nhid->nhjd", score_grad, queries, preferred_element_type=jnp.float32
    )
    bias_grad = jnp.sum(score_grad, 0, dtype=jnp.float32)
    table_grad = jax.ops.segment_sum(
        bias_grad.transpose(1, 2, 0).reshape(-1, head_local),
        offset_index.reshape(-1),
        num_segments=REL,
    )
    joined_grad = jnp.stack(
        [
            from_windows((query_grad * scale).astype(jnp.bfloat16), head_local),
            from_windows(key_grad.astype(jnp.bfloat16), head_local),
            from_windows(value_grad.astype(jnp.bfloat16), head_local),
        ],
        axis=1,
    ).reshape(image_tokens, 3 * head_width)
    joined_all = gradient_collect(joined_grad)
    joined_weight_grad = lax.dot_general(
        spread_one, joined_all, ROW_DIMS, preferred_element_type=jnp.float32
    ).reshape(-1, 3, head_width)
    column_totals = jnp.sum(joined_all, 0, dtype=jnp.float32).reshape(3, head_width)
    query_value_grad = jnp.stack([column_totals[0], column_totals[2]])
    normed_grad_one = token_back(joined_all, joined_weight, local_tokens)
    first_gain_grad = jnp.sum(normed_grad_one * normed_one, 0)
    first_shift_grad = jnp.sum(normed_grad_one, 0)
    input_gradient = residual_grad + norm_backward(
        normed_grad_one, normed_one, inverse_one, first_gain, width
    )
    summed_weights = lax.psum(
        (
            pair_joined(joined_weight_grad),
            query_value_grad,
            pair_local(output_grad),
            output_bias_grad,
            expand_grad,
            expand_bias_grad,
            pair_local(contract_grad),
            contract_bias_grad,
        ),
        "dp",
    )
    summed_norms = lax.psum(
        (first_gain_grad, first_shift_grad, second_gain_grad, second_shift_grad), ("dp", "col")
    )
    summed_table = lax.psum(table_grad, ("dp", "row"))
    return (
        pair_local(layer_output),
        pair_local(input_gradient),
        summed_norms[0],
        summed_norms[1],
        summed_weights[0],
        summed_weights[1],
        summed_table,
        summed_weights[2],
        summed_weights[3],
        summed_norms[2],
        summed_norms[3],
        summed_weights[4],
        summed_weights[5],
        summed_weights[6],
        summed_weights[7],
    )


def solution(mesh):
    in_specs = (
        P(("dp", "col"), "row", None),
        P(("dp", "col"), "row", None),
        P(),
        P(),
        P(),
        P("row"),
        P("row"),
        P("row", None, "col", None),
        P(None, "col"),
        P(None, "col"),
        P("col", "row", None),
        P("row"),
        P("row"),
        P("row"),
        P("row", "col"),
        P("col"),
        P("col", "row", None),
        P("row"),
    )
    out_specs = (
        P(("dp", "col"), "row", None),
        P(("dp", "col"), "row", None),
        P("row"),
        P("row"),
        P("row", None, "col", None),
        P(None, "col"),
        P(None, "col"),
        P("col", "row", None),
        P("row"),
        P("row"),
        P("row"),
        P("row", "col"),
        P("col"),
        P("col", "row", None),
        P("row"),
    )
    return jax.shard_map(local, mesh=mesh, in_specs=in_specs, out_specs=out_specs, check_vma=False)
```

profile of v0, /device:TPU:0, one launch (start us, length us, event | category | flops | bytes accessed | tf_op | source)
XLA Modules:
  0.0 1180.4 jit_solution(9655379731013944303)
XLA Ops:
  9.7 13.7 %all-reduce.4 = (f32[576]{0:T(1024)S(1)}, f32[576]{0:T(1024)S(1)}) all-reduce(f32[576]{0:T(1024)S(1)} %get-tuple-element.101, f32[576]{0:T(1024)S(1)} %get-tuple-element.100), channel_id=1, replica_groups=mesh['dp'=2,'row'=4,'col'=4] {'row'}, use_global_device_ids=true, to_apply=%region_3.4 | all-reduce | flops 1152 | bytes 9216 | tf_op jit(solution)/shard_map/psum | solution.py:71
  23.8 9.7 all-gather
  41.0 39.4 %gather_fusion = f32[20736,6]{1,0:T(8,128)} fusion(f32[529,6]{1,0:T(8,128)S(1)} %copy.285, s32[21504]{0:T(1024)S(1)} %pad_clamp_fusion), kind=kCustom, calls=%fused_computation | custom fusion | bytes 1078272 | tf_op jit(solution)/shard_map/jit(_take)/gather | solution.py:206
  80.4 11.6 copy.286
  94.1 46.5 %reduce-scatter.19.cloned.1.call-done = f32[576,576]{1,0:T(8,128)} async-done(((f32[2304,576]{1,0:T(8,128)}), f32[576,576]{1,0:T(8,128)}) %reduce-scatter.19.cloned.1.call-update) | async-done | bytes 1327120 | tf_op jit(solution)/shard_map/reduce_scatter | solution.py:112
  212.2 21.2 %all-gather.1 = bf16[4,576,192]{1,2,0:T(8,128)(2,1)S(1)} all-gather(bf16[1,576,192]{1,2,0:T(8,128)(2,1)S(1)} %reshape.291), channel_id=1, replica_groups=mesh['dp'=2,'row'=4,'col'=4] {'row'}, dimensions={0}, use_global_device_ids=true | all-gather | bytes 1105920 | tf_op jit(solution)/shard_map/all_gather | solution.py:96
  241.9 9.9 all-gather.3
  255.6 4.1 fusion.41
  259.7 13.0 %reduce-scatter.25.cloned.1.call-done = f32[576,192]{1,0:T(8,128)} async-done(((f32[2304,192]{1,0:T(8,128)}), f32[576,192]{1,0:T(8,128)}) %reduce-scatter.25.cloned.1.call-update) | async-done | bytes 442384 | tf_op jit(solution)/shard_map/reduce_scatter | solution.py:125
  274.0 12.0 %all-reduce.3 = (f32[576]{0:T(1024)S(1)}, f32[576]{0:T(1024)S(1)}) all-reduce(f32[576]{0:T(1024)S(1)} %get-tuple-element.99, f32[576]{0:T(1024)S(1)} %get-tuple-element.98), channel_id=1, replica_groups=mesh['dp'=2,'row'=4,'col'=4] {'row'}, use_global_device_ids=true, to_apply=%region_11.12 | all-reduce | flops 1152 | bytes 9216 | tf_op jit(solution)/shard_map/psum | solution.py:71
  287.2 8.7 all-gather.2
  299.7 4.1 fusion.39
  304.2 94.6 %reduce-scatter.23.cloned.1.call-done = f32[576,768]{1,0:T(8,128)} async-done(((f32[2304,768]{1,0:T(8,128)}), f32[576,768]{1,0:T(8,128)}) %reduce-scatter.23.cloned.1.call-update) | async-done | bytes 1769488 | tf_op jit(solution)/shard_map/reduce_scatter | solution.py:138
  398.8 126.1 %reduce-scatter.21.cloned.1.call-done = f32[576,768]{1,0:T(8,128)} async-done(((f32[2304,768]{1,0:T(8,128)}), f32[576,768]{1,0:T(8,128)}) %reduce-scatter.21.cloned.1.call-update) | async-done | bytes 1769488 | tf_op jit(solution)/shard_map/reduce_scatter | solution.py:112
  525.0 6.8 add_convert_fusion.1
  535.1 67.4 %all-gather.11.cloned.1.call-done = bf16[2304,768]{1,0:T(8,128)(2,1)} async-done(((bf16[576,768]{1,0:T(8,128)(2,1)}), bf16[2304,768]{1,0:T(8,128)(2,1)}) %all-gather.11.cloned.1.call-update) | async-done | bytes 3538960 | tf_op jit(solution)/shard_map/all_gather | solution.py:104
  602.5 4.6 fusion.42
  607.1 65.5 %all-gather.9.cloned.1.call-done = bf16[2304,768]{1,0:T(8,128)(2,1)} async-done(((bf16[576,768]{1,0:T(8,128)(2,1)}), bf16[2304,768]{1,0:T(8,128)(2,1)}) %all-gather.9.cloned.1.call-update) | async-done | bytes 3538960 | tf_op jit(solution)/shard_map/all_gather | solution.py:96
  672.6 4.5 fusion.40
  677.1 29.8 %reduce-scatter.29.cloned.1.call-done = f32[576,192]{1,0:T(8,128)} async-done(((f32[2304,192]{1,0:T(8,128)}), f32[576,192]{1,0:T(8,128)}) %reduce-scatter.29.cloned.1.call-update) | async-done | bytes 442384 | tf_op jit(solution)/shard_map/reduce_scatter | solution.py:151
  709.0 11.8 %all-reduce.2 = (f32[576]{0:T(1024)S(1)}, f32[576]{0:T(1024)S(1)}) all-reduce(f32[576]{0:T(1024)S(1)} %get-tuple-element.91, f32[576]{0:T(1024)S(1)} %get-tuple-element.95), channel_id=1, replica_groups=mesh['dp'=2,'row'=4,'col'=4] {'row'}, use_global_device_ids=true, to_apply=%region_20.21 | all-reduce | flops 1152 | bytes 9216 | tf_op jit(solution)/shard_map/psum | solution.py:71
  721.5 21.1 %reduce-scatter.27.cloned.1.call-done = f32[576,192]{1,0:T(8,128)} async-done(((f32[2304,192]{1,0:T(8,128)}), f32[576,192]{1,0:T(8,128)}) %reduce-scatter.27.cloned.1.call-update) | async-done | bytes 442384 | tf_op jit(solution)/shard_map/reduce_scatter | solution.py:125
  745.4 9.3 all-gather.4
  761.3 47.8 %reduce-scatter.31.cloned.1.call-done = f32[576,192]{1,0:T(8,128)} async-done(((f32[2304,192]{1,0:T(8,128)}), f32[576,192]{1,0:T(8,128)}) %reduce-scatter.31.cloned.1.call-update) | async-done | bytes 442384
  896.1 4.3 fusion.46
  901.7 48.1 %all-gather.13.cloned.1.call-done = bf16[2304,576]{1,0:T(8,128)(2,1)} async-done(((bf16[576,576]{1,0:T(8,128)(2,1)}), bf16[2304,576]{1,0:T(8,128)(2,1)}) %all-gather.13.cloned.1.call-update) | async-done | bytes 2654224 | tf_op jit(solution)/shard_map/all_gather | solution.py:104
  969.0 11.2 copy.342
  980.2 113.1 %scatter_custom_fusion = f32[529,6]{1,0:T(8,128)} fusion(s32[20736]{0:T(1024)} %reshape.280, f32[20736,6]{1,0:T(8,128)} %bitcast.156, f32[]{:T(128)} %constant.48.clone.1), kind=kCustom, calls=%fused_computation.94 | custom fusion | flops 124416 | bytes 13208 | tf_op jit(solution)/shard_map/scatter-add | solution.py:297
  1093.3 40.7 %psum.159 = f32[529,6]{1,0:T(8,128)S(1)} all-reduce(f32[529,6]{1,0:T(8,128)} %scatter_custom_fusion), channel_id=1, replica_groups=mesh['dp'=2,'row'=4,'col'=4] {'dp','row'}, use_global_device_ids=true, to_apply=%region_37.38 | all-reduce | flops 3174 | bytes 25392 | tf_op jit(solution)/shard_map/psum | solution.py:338
  1135.4 5.7 all-reduce.5
  1147.4 9.2 all-reduce.1
  1159.4 12.4 %all-reduce = (f32[192]{0:T(256)}, f32[192]{0:T(256)}, f32[192]{0:T(256)}, f32[192]{0:T(256)}) all-reduce(f32[192]{0:T(256)S(1)} %get-tuple-element.92, f32[192]{0:T(256)S(1)} %get-tuple-element.97, f32[192]{0:T(256)S(1)} %copy-done.51, f32[192]{0:T(256)S(1)} %copy-done.52), channel_id=1, replica_groups=mesh['dp'=2,'row'=4,'col'=4] {'dp','col'}, use_global_device_ids=true, to_apply=%region_29.30 | all-reduce | flops 768 | bytes 6144 | tf_op jit(solution)/shard_map/psum | solution.py:335
  (311 shorter events, 237.1 us)
Async XLA Ops:
  7.2 292.5 %copy-start = (bf16[192,768]{1,0:T(8,128)(2,1)S(1)}, bf16[192,768]{1,0:T(8,128)(2,1)}, u32[]{:S(2)}) copy-start(bf16[192,768]{1,0:T(8,128)(2,1)} %param.32) | copy-start | bytes 884740
  7.2 16.2 %copy-start.47 = (f32[192]{0:T(256)S(1)}, f32[192]{0:T(256)}, u32[]{:S(2)}) copy-start(f32[192]{0:T(256)} %param.23) | copy-start | bytes 2308
  7.2 16.2 %copy-start.54 = (f32[192]{0:T(256)S(1)}, f32[192]{0:T(256)}, u32[]{:S(2)}) copy-start(f32[192]{0:T(256)} %param.24) | copy-start | bytes 2308
  7.2 133.3 %reduce-scatter.19.cloned.1.call-start = ((), (), s32[]{:S(2)}) async-start(), calls=%async_computation.8 | async-start | bytes 7372800 | tf_op jit(solution)/shard_map/reduce_scatter | solution.py:112
  9.3 25.8 %copy-start.24 = (bf16[192,576]{1,0:T(8,128)(2,1)}, bf16[192,576]{1,0:T(8,128)(2,1)S(1)}, u32[]{:S(2)}) copy-start(bf16[192,576]{1,0:T(8,128)(2,1)S(1)} %reshape_reshape.6) | copy-start | bytes 663556
  9.4 263.3 %copy-start.4 = (f32[576,192]{1,0:T(8,128)}, f32[576,192]{1,0:T(8,128)S(1)}, u32[]{:S(2)}) copy-start(f32[576,192]{1,0:T(8,128)S(1)} %reshape.268) | copy-start | bytes 1327108
  38.7 234.0 %reduce-scatter.25.cloned.1.call-start = ((), (), s32[]{:S(2)}) async-start(), calls=%async_computation.14 | async-start | bytes 2949120 | tf_op jit(solution)/shard_map/reduce_scatter | solution.py:125
  239.3 159.5 %reduce-scatter.23.cloned.1.call-start = ((), (), s32[]{:S(2)}) async-start(), calls=%async_computation.11 | async-start | bytes 8847360 | tf_op jit(solution)/shard_map/reduce_scatter | solution.py:138
  240.1 11.7 copy-start.43
  241.3 14.2 %copy-start.17 = (bf16[768,192]{1,0:T(8,128)(2,1)}, bf16[768,192]{1,0:T(8,128)(2,1)S(1)}, u32[]{:S(2)}) copy-start(bf16[768,192]{1,0:T(8,128)(2,1)S(1)} %reshape.251) | copy-start | bytes 884740
  255.6 634.4 %copy-start.9 = (bf16[2304,192]{0,1:T(8,128)(2,1)}, bf16[2304,192]{0,1:T(8,128)(2,1)S(1)}, u32[]{:S(2)}) copy-start(bf16[2304,192]{0,1:T(8,128)(2,1)S(1)} %reshape.296) | copy-start | bytes 2654212
  259.6 13.0 %copy-start.55 = (f32[192]{0:T(256)S(1)}, f32[192]{0:T(256)}, u32[]{:S(2)}) copy-start(f32[192]{0:T(256)} %param.29) | copy-start | bytes 2308
  259.7 26.4 %copy-start.49 = (f32[192]{0:T(256)S(1)}, f32[192]{0:T(256)}, u32[]{:S(2)}) copy-start(f32[192]{0:T(256)} %param.30) | copy-start | bytes 2308
  259.7 265.3 %reduce-scatter.21.cloned.1.call-start = ((), (), s32[]{:S(2)}) async-start(), calls=%async_computation.9 | async-start | bytes 8847360 | tf_op jit(solution)/shard_map/reduce_scatter | solution.py:112
  303.7 221.2 %copy-start.45 = (f32[768]{0:T(1024)S(1)}, f32[768]{0:T(1024)}, u32[]{:S(2)}) copy-start(f32[768]{0:T(1024)} %param.33) | copy-start | bytes 9220
  303.8 298.7 %all-gather.11.cloned.1.call-start = ((), (), s32[]{:S(2)}) async-start(), calls=%async_computation.12 | async-start | bytes 4423680 | tf_op jit(solution)/shard_map/all_gather | solution.py:104
  531.8 140.8 %all-gather.9.cloned.1.call-start = ((), (), s32[]{:S(2)}) async-start(), calls=%async_computation.10 | async-start | bytes 4423680 | tf_op jit(solution)/shard_map/all_gather | solution.py:96
  535.0 171.9 %reduce-scatter.29.cloned.1.call-start = ((), (), s32[]{:S(2)}) async-start(), calls=%async_computation.16 | async-start | bytes 2949120 | tf_op jit(solution)/shard_map/reduce_scatter | solution.py:151
  607.0 65.5 %copy-start.18 = (bf16[768,192]{1,0:T(8,128)(2,1)S(1)}, bf16[768,192]{1,0:T(8,128)(2,1)}, u32[]{:S(2)}) copy-start(bf16[768,192]{1,0:T(8,128)(2,1)} %copy-done.17) | copy-start | bytes 884740
  607.1 135.5 %reduce-scatter.27.cloned.1.call-start = ((), (), s32[]{:S(2)}) async-start(), calls=%async_computation.15 | async-start | bytes 2949120 | tf_op jit(solution)/shard_map/reduce_scatter | solution.py:125
  677.1 29.9 %copy-start.50 = (f32[192]{0:T(256)S(1)}, f32[192]{0:T(256)}, u32[]{:S(2)}) copy-start(f32[192]{0:T(256)} %param.30) | copy-start | bytes 2308
  677.1 65.5 %copy-start.14 = (f32[576,192]{1,0:T(8,128)S(1)}, f32[576,192]{1,0:T(8,128)}, u32[]{:S(2)}) copy-start(f32[576,192]{1,0:T(8,128)} %copy-done.13) | copy-start | bytes 1327108
  677.1 132.1 %reduce-scatter.31.cloned.1.call-start = ((), (), s32[]{:S(2)}) async-start(), calls=%async_computation.17 | async-start | bytes 2949120
  758.4 141.9 %copy-start.6 = (bf16[2304,192]{0,1:T(8,128)(2,1)}, bf16[2304,192]{0,1:T(8,128)(2,1)S(1)}, u32[]{:S(2)}) copy-start(bf16[2304,192]{0,1:T(8,128)(2,1)S(1)} %reshape.298) | copy-start | bytes 2654212
  760.6 189.2 %all-gather.13.cloned.1.call-start = ((), (), s32[]{:S(2)}) async-start(), calls=%async_computation.13 | async-start | bytes 3686400 | tf_op jit(solution)/shard_map/all_gather | solution.py:104
  889.9 251.2 %all-reduce.9.cloned.1.call-start = ((), (), s32[]{:S(2)}) async-start(), calls=%async_computation.19 | async-start | bytes 3538944 | tf_op jit(solution)/shard_map/psum | solution.py:322
  958.4 187.4 %reduce-scatter.33.cloned.1.call-start = ((), (), s32[]{:S(2)}) async-start(), calls=%async_computation.18 | async-start | bytes 2949120 | tf_op jit(solution)/shard_map/reduce_scatter | solution.py:151
  1135.3 21.3 %copy-start.23 = (f32[576,192]{1,0:T(8,128)S(1)}, f32[576,192]{1,0:T(8,128)}, u32[]{:S(2)}) copy-start(f32[576,192]{1,0:T(8,128)} %get-tuple-element.127) | copy-start | bytes 1327108
  1147.3 12.1 %copy-start.51 = (f32[192]{0:T(256)S(1)}, f32[192]{0:T(256)}, u32[]{:S(2)}) copy-start(f32[192]{0:T(256)} %get-tuple-element.90) | copy-start | bytes 2308
  1147.3 12.1 %copy-start.52 = (f32[192]{0:T(256)S(1)}, f32[192]{0:T(256)}, u32[]{:S(2)}) copy-start(f32[192]{0:T(256)} %get-tuple-element.96) | copy-start | bytes 2308
  1147.4 24.4 %copy-start.39 = (f32[96,1,384]{2,1,0:T(1,128)S(1)}, f32[96,1,384]{2,1,0:T(1,128)}, u32[]{:S(2)}) copy-start(f32[96,1,384]{2,1,0:T(1,128)} %get-tuple-element.153) | copy-start | bytes 442372
  1156.6 15.9 %copy-start.34 = (f32[192,768]{1,0:T(8,128)S(1)}, f32[192,768]{1,0:T(8,128)}, u32[]{:S(2)}) copy-start(f32[192,768]{1,0:T(8,128)} %get-tuple-element.157) | copy-start | bytes 1769476
  (43 other events, 120.9 us)
Sparse Core Ops, SparseCore 0:
  38.8 101.6 reduce-scatter.18
  239.4 33.2 reduce-scatter.24
  275.1 123.6 reduce-scatter.22
  401.1 123.8 reduce-scatter.20
  531.9 70.4 all-gather.10
  604.0 68.5 all-gather.8
  675.3 31.6 reduce-scatter.28
  709.5 33.0 reduce-scatter.26
  760.7 48.4 reduce-scatter.30
  890.0 59.7 all-gather.12
  958.5 54.9 all-reduce.8
  1015.9 33.0 reduce-scatter.32
where the time goes:
time: 1190 us; the launch traced here: 1180 us
  waiting for transfers between devices  560 us (47%)
  local copies, waits for them, and re-layouts  217 us (18%)
  other arithmetic  172 us (14%)
  blocking collectives  164 us (14%)
  matrix products  50.2 us (4%)
  between operations  15.4 us (1%)
    reduce_scatter x2, waiting for transfers between devices, width_sums(): lax.psum_scatter(partial_rows(jnp.int32(0), lax.axis_size('row') * row_co...  173 us
    all_gather x2, waiting for transfers between devices, gradient_collect(): return lax.all_gather(values, 'row', axis=0, tiled=True)  115 us
    scatter-add x1, other arithmetic, local(): jax.ops.segment_sum(bias_grad.transpose(1, 2, 0).reshape(-1, head_local),...  113 us
    reduce_scatter x1, waiting for transfers between devices, width_back(): lax.psum_scatter(partial_rows(jnp.int32(0), lax.axis_size('row') * row_co...  94.6 us
    all_gather x1, waiting for transfers between devices, head_collect(): return lax.all_gather(values, 'row', axis=0, tiled=True)  65.5 us
    gather x2, local copies, waits for them, and re-layouts, local(): jnp.take(position_table, offset_index, axis=0).transpose(2, 0, 1)  51.1 us
    unnamed x13, waiting for transfers between devices  48 us
    psum x4, blocking collectives, norm_totals(): return lax.psum((jnp.sum(first_term, -1), jnp.sum(second_term, -1)), 'row')  46.8 us
  transfers between devices with their start and end apart: 12, of which 10 were waited for; matrix products, arithmetic and copies ran while one was open for 20% of the time, Pallas kernels for 0%

commit v1 on v0

--- a/solution.py
+++ b/solution.py
@@ -1,3 +1,4 @@
+import functools
 import jax
 import jax.numpy as jnp
 from jax import lax
@@ -14,6 +15,27 @@
 ROW_DIMS = (((0,), (0,)), ((), ()))
 
 
+def entries_register(row_data, row_dim):
+    raw_out, row_out, val2 = (
+        jax.lax.psum(1, axis_name="row"),
+        jax.lax.axis_index("row"),
+        row_data.shape[row_dim],
+    )
+    base_arr, odd = (row_data, 1)
+    while odd < raw_out:
+        grid = []
+        for u in range(raw_out):
+            grid.append((u, (u - odd) % raw_out))
+        base_arr = jnp.concatenate(
+            [base_arr, jax.lax.ppermute(base_arr, axis_name="row", perm=grid)], axis=row_dim
+        )
+        odd = 2 * odd
+    return jnp.roll(base_arr, row_out * val2, axis=row_dim)
+
+
+meet_the_series = functools.partial(entries_register, row_dim=0)
+
+
 def unpair_local(paired):
     return paired.reshape(paired.shape[0] * 2, paired.shape[2] // 2)
 
@@ -93,7 +115,7 @@
 
 
 def head_collect(values):
-    return lax.all_gather(values, "row", axis=0, tiled=True)
+    return meet_the_series(values)
 
 
 def cotangent_spread(values):

time: 1190 us -> 1200 us (level)
  blocking collectives: 164 us -> 142 us
  waiting for transfers between devices: 560 us -> 577 us
    ppermute x0 -> x4, waiting for transfers between devices: none -> 101 us  [entries_register(): jax.lax.ppermute(base_arr, axis_name='row', perm=grid)]
    all_gather x1 -> x0, waiting for transfers between devices: 65.5 us -> none  [head_collect(): return lax.all_gather(values, 'row', axis=0, tiled=True)]
    reduce_scatter x2, waiting for transfers between devices: 29.8 us -> 0.02 us  [token_back(): lax.psum_scatter(partial_rows(jnp.int32(0), lax.axis_size('col') * row_co...]
    all_gather x1 -> x0, blocking collectives: 21.2 us -> none  [head_collect(): return lax.all_gather(values, 'row', axis=0, tiled=True)]
    unnamed x131 -> x133, local copies, waits for them, and re-layouts: 24.2 us -> 27.6 us
    unnamed x13 -> x12, waiting for transfers between devices: 48 us -> 48 us
  transfers between devices with their start and end apart: 12 -> 15, of which waited for: 10 -> 11; matrix products, arithmetic and copies ran while one was open for 20% -> 21% of each run, Pallas kernels for 0% -> 0%
where the time goes in v1:
time: 1200 us; the launch traced here: 1190 us
  waiting for transfers between devices  577 us (48%)
  local copies, waits for them, and re-layouts  222 us (18%)
  other arithmetic  174 us (14%)
  blocking collectives  142 us (12%)
  matrix products  52.1 us (4%)
  between operations  15.1 us (1%)
    reduce_scatter x2, waiting for transfers between devices, width_sums(): lax.psum_scatter(partial_rows(jnp.int32(0), lax.axis_size('row') * row_co...  173 us
    all_gather x2, waiting for transfers between devices, gradient_collect(): return lax.all_gather(values, 'row', axis=0, tiled=True)  126 us
    scatter-add x1, other arithmetic, local(): jax.ops.segment_sum(bias_grad.transpose(1, 2, 0).reshape(-1, head_local),...  113 us
    ppermute x4, waiting for transfers between devices, entries_register(): jax.lax.ppermute(base_arr, axis_name='row', perm=grid)  101 us
    reduce_scatter x1, waiting for transfers between devices, width_back(): lax.psum_scatter(partial_rows(jnp.int32(0), lax.axis_size('row') * row_co...  94.9 us
    gather x2, local copies, waits for them, and re-layouts, local(): jnp.take(position_table, offset_index, axis=0).transpose(2, 0, 1)  51.1 us
    unnamed x12, waiting for transfers between devices  48 us
    psum x4, blocking collectives, norm_totals(): return lax.psum((jnp.sum(first_term, -1), jnp.sum(second_term, -1)), 'row')  46.2 us
  transfers between devices with their start and end apart: 15, of which 11 were waited for; matrix products, arithmetic and copies ran while one was open for 21% of the time, Pallas kernels for 0%

profile of v1, /device:TPU:0, one launch (start us, length us, event | category | flops | bytes accessed | tf_op | source)
XLA Modules:
  0.0 1192.7 jit_solution(622109002659441809)
XLA Ops:
  9.7 13.7 %all-reduce.4 = (f32[576]{0:T(1024)S(1)}, f32[576]{0:T(1024)S(1)}) all-reduce(f32[576]{0:T(1024)S(1)} %get-tuple-element.101, f32[576]{0:T(1024)S(1)} %get-tuple-element.100), channel_id=1, replica_groups=mesh['dp'=2,'row'=4,'col'=4] {'row'}, use_global_device_ids=true, to_apply=%region_3.4 | all-reduce | flops 1152 | bytes 9216 | tf_op jit(solution)/shard_map/psum | solution.py:93
  23.8 9.7 all-gather
  40.2 39.4 %gather_fusion = f32[20736,6]{1,0:T(8,128)} fusion(f32[529,6]{1,0:T(8,128)S(1)} %copy.282, s32[21504]{0:T(1024)S(1)} %pad_clamp_fusion), kind=kCustom, calls=%fused_computation | custom fusion | bytes 1078272 | tf_op jit(solution)/shard_map/jit(_take)/gather | solution.py:228
  79.7 11.6 copy.283
  93.3 47.2 %reduce-scatter.19.cloned.1.call-done = f32[576,576]{1,0:T(8,128)} async-done(((f32[2304,576]{1,0:T(8,128)}), f32[576,576]{1,0:T(8,128)}) %reduce-scatter.19.cloned.1.call-update) | async-done | bytes 1327120 | tf_op jit(solution)/shard_map/reduce_scatter | solution.py:134
  214.7 5.4 collective-permute-done
  223.1 18.8 %collective-permute-done.1 = bf16[1152,192]{0,1:T(8,128)(2,1)S(1)} collective-permute-done((bf16[1152,192]{0,1:T(8,128)(2,1)S(1)}, bf16[1152,192]{0,1:T(8,128)(2,1)S(1)}, u32[]{:S(2)}, u32[]{:S(2)}) %collective-permute-start.1) | collective-permute-done | bytes 442400 | tf_op jit(solution)/shard_map/ppermute | solution.py:30
  249.8 9.5 all-gather.2
  263.2 4.1 fusion.51
  267.4 14.9 %reduce-scatter.25.cloned.1.call-done = f32[576,192]{1,0:T(8,128)} async-done(((f32[2304,192]{1,0:T(8,128)}), f32[576,192]{1,0:T(8,128)}) %reduce-scatter.25.cloned.1.call-update) | async-done | bytes 442384 | tf_op jit(solution)/shard_map/reduce_scatter | solution.py:147
  283.7 12.0 %all-reduce.3 = (f32[576]{0:T(1024)S(1)}, f32[576]{0:T(1024)S(1)}) all-reduce(f32[576]{0:T(1024)S(1)} %get-tuple-element.99, f32[576]{0:T(1024)S(1)} %get-tuple-element.98), channel_id=1, replica_groups=mesh['dp'=2,'row'=4,'col'=4] {'row'}, use_global_device_ids=true, to_apply=%region_11.12 | all-reduce | flops 1152 | bytes 9216 | tf_op jit(solution)/shard_map/psum | solution.py:93
  296.8 8.7 all-gather.1
  309.3 4.1 fusion.50
  313.5 94.9 %reduce-scatter.23.cloned.1.call-done = f32[576,768]{1,0:T(8,128)} async-done(((f32[2304,768]{1,0:T(8,128)}), f32[576,768]{1,0:T(8,128)}) %reduce-scatter.23.cloned.1.call-update) | async-done | bytes 1769488 | tf_op jit(solution)/shard_map/reduce_scatter | solution.py:160
  408.4 126.1 %reduce-scatter.21.cloned.1.call-done = f32[576,768]{1,0:T(8,128)} async-done(((f32[2304,768]{1,0:T(8,128)}), f32[576,768]{1,0:T(8,128)}) %reduce-scatter.21.cloned.1.call-update) | async-done | bytes 1769488 | tf_op jit(solution)/shard_map/reduce_scatter | solution.py:134
  534.6 6.8 add_convert_fusion.1
  547.9 77.7 %all-gather.7.cloned.1.call-done = bf16[2304,768]{1,0:T(8,128)(2,1)} async-done(((bf16[576,768]{1,0:T(8,128)(2,1)}), bf16[2304,768]{1,0:T(8,128)(2,1)}) %all-gather.7.cloned.1.call-update) | async-done | bytes 3538960 | tf_op jit(solution)/shard_map/all_gather | solution.py:126
  625.7 4.5 fusion.52
  634.5 76.5 %collective-permute-done.3 = bf16[1152,768]{1,0:T(8,128)(2,1)S(1)} collective-permute-done((bf16[1152,768]{1,0:T(8,128)(2,1)S(1)}, bf16[1152,768]{1,0:T(8,128)(2,1)S(1)}, u32[]{:S(2)}, u32[]{:S(2)}) %collective-permute-start.3) | collective-permute-done | bytes 1769504 | tf_op jit(solution)/shard_map/ppermute | solution.py:30
  716.9 4.5 fusion.3
  724.1 11.3 all-reduce.2
  736.1 18.9 %reduce-scatter.27.cloned.1.call-done = f32[576,192]{1,0:T(8,128)} async-done(((f32[2304,192]{1,0:T(8,128)}), f32[576,192]{1,0:T(8,128)}) %reduce-scatter.27.cloned.1.call-update) | async-done | bytes 442384 | tf_op jit(solution)/shard_map/reduce_scatter | solution.py:147
  757.7 9.3 all-gather.3
  773.7 47.8 %reduce-scatter.31.cloned.1.call-done = f32[576,192]{1,0:T(8,128)} async-done(((f32[2304,192]{1,0:T(8,128)}), f32[576,192]{1,0:T(8,128)}) %reduce-scatter.31.cloned.1.call-update) | async-done | bytes 442384
  908.7 4.4 fusion.55
  914.4 47.9 %all-gather.9.cloned.1.call-done = bf16[2304,576]{1,0:T(8,128)(2,1)} async-done(((bf16[576,576]{1,0:T(8,128)(2,1)}), bf16[2304,576]{1,0:T(8,128)(2,1)}) %all-gather.9.cloned.1.call-update) | async-done | bytes 2654224 | tf_op jit(solution)/shard_map/all_gather | solution.py:126
  981.6 11.3 copy.338
  992.9 113.3 %scatter_custom_fusion = f32[529,6]{1,0:T(8,128)} fusion(s32[20736]{0:T(1024)} %reshape.280, f32[20736,6]{1,0:T(8,128)} %bitcast.150, f32[]{:T(128)} %constant.51.clone.1), kind=kCustom, calls=%fused_computation.104 | custom fusion | flops 124416 | bytes 13208 | tf_op jit(solution)/shard_map/scatter-add | solution.py:319
  1106.3 40.5 %psum.159 = f32[529,6]{1,0:T(8,128)S(1)} all-reduce(f32[529,6]{1,0:T(8,128)} %scatter_custom_fusion), channel_id=1, replica_groups=mesh['dp'=2,'row'=4,'col'=4] {'dp','row'}, use_global_device_ids=true, to_apply=%region_37.38 | all-reduce | flops 3174 | bytes 25392 | tf_op jit(solution)/shard_map/psum | solution.py:360
  1148.1 5.7 all-reduce.5
  1160.1 9.1 all-reduce.1
  1172.1 12.4 %all-reduce = (f32[192]{0:T(256)}, f32[192]{0:T(256)}, f32[192]{0:T(256)}, f32[192]{0:T(256)}) all-reduce(f32[192]{0:T(256)S(1)} %get-tuple-element.92, f32[192]{0:T(256)S(1)} %get-tuple-element.97, f32[192]{0:T(256)S(1)} %copy-done.51, f32[192]{0:T(256)S(1)} %copy-done.52), channel_id=1, replica_groups=mesh['dp'=2,'row'=4,'col'=4] {'dp','col'}, use_global_device_ids=true, to_apply=%region_29.30 | all-reduce | flops 768 | bytes 6144 | tf_op jit(solution)/shard_map/psum | solution.py:357
  (321 shorter events, 255.1 us)
Async XLA Ops:
  7.2 302.1 %copy-start = (bf16[192,768]{1,0:T(8,128)(2,1)S(1)}, bf16[192,768]{1,0:T(8,128)(2,1)}, u32[]{:S(2)}) copy-start(bf16[192,768]{1,0:T(8,128)(2,1)} %param.32) | copy-start | bytes 884740
  7.2 16.2 %copy-start.47 = (f32[192]{0:T(256)S(1)}, f32[192]{0:T(256)}, u32[]{:S(2)}) copy-start(f32[192]{0:T(256)} %param.23) | copy-start | bytes 2308
  7.2 16.2 %copy-start.54 = (f32[192]{0:T(256)S(1)}, f32[192]{0:T(256)}, u32[]{:S(2)}) copy-start(f32[192]{0:T(256)} %param.24) | copy-start | bytes 2308
  7.2 133.3 %reduce-scatter.19.cloned.1.call-start = ((), (), s32[]{:S(2)}) async-start(), calls=%async_computation.8 | async-start | bytes 7372800 | tf_op jit(solution)/shard_map/reduce_scatter | solution.py:134
  9.3 25.8 %copy-start.21 = (bf16[192,576]{1,0:T(8,128)(2,1)}, bf16[192,576]{1,0:T(8,128)(2,1)S(1)}, u32[]{:S(2)}) copy-start(bf16[192,576]{1,0:T(8,128)(2,1)S(1)} %reshape_reshape.6) | copy-start | bytes 663556
  9.4 272.9 %copy-start.4 = (f32[576,192]{1,0:T(8,128)}, f32[576,192]{1,0:T(8,128)S(1)}, u32[]{:S(2)}) copy-start(f32[576,192]{1,0:T(8,128)S(1)} %reshape.268) | copy-start | bytes 1327108
  38.7 243.6 %reduce-scatter.25.cloned.1.call-start = ((), (), s32[]{:S(2)}) async-start(), calls=%async_computation.13 | async-start | bytes 2949120 | tf_op jit(solution)/shard_map/reduce_scatter | solution.py:147
  209.5 13.5 %copy-start.42 = (bf16[96,1,384]{2,0,1:T(8,128)(2,1)S(1)}, bf16[96,1,384]{2,0,1:T(8,128)(2,1)}, u32[]{:S(2)}) copy-start(bf16[96,1,384]{2,0,1:T(8,128)(2,1)} %param.28) | copy-start | bytes 221188
  212.1 8.1 collective-permute-start
  220.3 21.7 %collective-permute-start.1 = (bf16[1152,192]{0,1:T(8,128)(2,1)S(1)}, bf16[1152,192]{0,1:T(8,128)(2,1)S(1)}, u32[]{:S(2)}, u32[]{:S(2)}) collective-permute-start(bf16[1152,192]{0,1:T(8,128)(2,1)S(1)} %pad_maximum_fusion.14), channel_id=1, source_target_pairs={{0,8},{4,12},{8,0},{12,4},{1,9},{5,13},{9,1},{13,5},{2,10},{6,14},... | collective-permute-start | bytes 1327112 | tf_op jit(solution)/shard_map/ppermute | solution.py:30
  223.1 21.2 %copy-start.31 = (bf16[192,192]{1,0:T(8,128)(2,1)}, bf16[192,192]{1,0:T(8,128)(2,1)S(1)}, u32[]{:S(2)}) copy-start(bf16[192,192]{1,0:T(8,128)(2,1)S(1)} %reshape.250) | copy-start | bytes 221188
  248.1 160.3 %reduce-scatter.23.cloned.1.call-start = ((), (), s32[]{:S(2)}) async-start(), calls=%async_computation.10 | async-start | bytes 8847360 | tf_op jit(solution)/shard_map/reduce_scatter | solution.py:160
  249.3 13.9 %copy-start.24 = (bf16[768,192]{1,0:T(8,128)(2,1)}, bf16[768,192]{1,0:T(8,128)(2,1)S(1)}, u32[]{:S(2)}) copy-start(bf16[768,192]{1,0:T(8,128)(2,1)S(1)} %reshape.251) | copy-start | bytes 884740
  263.2 639.3 %copy-start.9 = (bf16[2304,192]{0,1:T(8,128)(2,1)}, bf16[2304,192]{0,1:T(8,128)(2,1)S(1)}, u32[]{:S(2)}) copy-start(bf16[2304,192]{0,1:T(8,128)(2,1)S(1)} %reshape.294) | copy-start | bytes 2654212
  267.3 15.0 %copy-start.55 = (f32[192]{0:T(256)S(1)}, f32[192]{0:T(256)}, u32[]{:S(2)}) copy-start(f32[192]{0:T(256)} %param.29) | copy-start | bytes 2308
  267.3 28.4 %copy-start.49 = (f32[192]{0:T(256)S(1)}, f32[192]{0:T(256)}, u32[]{:S(2)}) copy-start(f32[192]{0:T(256)} %param.30) | copy-start | bytes 2308
  267.3 267.2 %reduce-scatter.21.cloned.1.call-start = ((), (), s32[]{:S(2)}) async-start(), calls=%async_computation.9 | async-start | bytes 8847360 | tf_op jit(solution)/shard_map/reduce_scatter | solution.py:134
  313.4 221.1 %copy-start.45 = (f32[768]{0:T(1024)S(1)}, f32[768]{0:T(1024)}, u32[]{:S(2)}) copy-start(f32[768]{0:T(1024)} %param.33) | copy-start | bytes 9220
  313.4 312.3 %all-gather.7.cloned.1.call-start = ((), (), s32[]{:S(2)}) async-start(), calls=%async_computation.11 | async-start | bytes 4423680 | tf_op jit(solution)/shard_map/all_gather | solution.py:126
  541.4 180.1 %reduce-scatter.29.cloned.1.call-start = ((), (), s32[]{:S(2)}) async-start(), calls=%async_computation.15 | async-start | bytes 2949120 | tf_op jit(solution)/shard_map/reduce_scatter | solution.py:173
  545.0 85.3 %collective-permute-start.2 = (bf16[576,768]{1,0:T(8,128)(2,1)}, bf16[576,768]{1,0:T(8,128)(2,1)S(1)}, u32[]{:S(2)}, u32[]{:S(2)}) collective-permute-start(bf16[576,768]{1,0:T(8,128)(2,1)} %get-tuple-element.131), channel_id=1, source_target_pairs={{0,12},{4,0},{8,4},{12,8},{1,13},{5,1},{9,5},{13,9},{2,14},{6,2},{... | collective-permute-start | bytes 2654216 | tf_op jit(solution)/shard_map/ppermute | solution.py:30
  630.3 124.7 %reduce-scatter.27.cloned.1.call-start = ((), (), s32[]{:S(2)}) async-start(), calls=%async_computation.14 | async-start | bytes 2949120 | tf_op jit(solution)/shard_map/reduce_scatter | solution.py:147
  631.6 79.5 %collective-permute-start.3 = (bf16[1152,768]{1,0:T(8,128)(2,1)S(1)}, bf16[1152,768]{1,0:T(8,128)(2,1)S(1)}, u32[]{:S(2)}, u32[]{:S(2)}) collective-permute-start(bf16[1152,768]{1,0:T(8,128)(2,1)S(1)} %pad_maximum_fusion), channel_id=1, source_target_pairs={{0,8},{4,12},{8,0},{12,4},{1,9},{5,13},{9,1},{13,5},{2,10},{6,14},... | collective-permute-start | bytes 5308424 | tf_op jit(solution)/shard_map/ppermute | solution.py:30
  721.4 33.6 %copy-start.13 = (f32[576,192]{1,0:T(8,128)S(1)}, f32[576,192]{1,0:T(8,128)}, u32[]{:S(2)}) copy-start(f32[576,192]{1,0:T(8,128)} %copy-done.12) | copy-start | bytes 1327108
  721.4 100.1 %reduce-scatter.31.cloned.1.call-start = ((), (), s32[]{:S(2)}) async-start(), calls=%async_computation.16 | async-start | bytes 2949120
  770.9 142.2 %copy-start.6 = (bf16[2304,192]{0,1:T(8,128)(2,1)}, bf16[2304,192]{0,1:T(8,128)(2,1)S(1)}, u32[]{:S(2)}) copy-start(bf16[2304,192]{0,1:T(8,128)(2,1)S(1)} %reshape.296) | copy-start | bytes 2654212
  772.9 189.4 %all-gather.9.cloned.1.call-start = ((), (), s32[]{:S(2)}) async-start(), calls=%async_computation.12 | async-start | bytes 3686400 | tf_op jit(solution)/shard_map/all_gather | solution.py:126
  902.4 251.5 %all-reduce.9.cloned.1.call-start = ((), (), s32[]{:S(2)}) async-start(), calls=%async_computation.18 | async-start | bytes 3538944 | tf_op jit(solution)/shard_map/psum | solution.py:344
  971.0 187.6 %reduce-scatter.33.cloned.1.call-start = ((), (), s32[]{:S(2)}) async-start(), calls=%async_computation.17 | async-start | bytes 2949120 | tf_op jit(solution)/shard_map/reduce_scatter | solution.py:173
  1148.1 21.1 %copy-start.20 = (f32[576,192]{1,0:T(8,128)S(1)}, f32[576,192]{1,0:T(8,128)}, u32[]{:S(2)}) copy-start(f32[576,192]{1,0:T(8,128)} %get-tuple-element.127) | copy-start | bytes 1327108
  1160.1 24.3 %copy-start.39 = (f32[96,1,384]{2,1,0:T(1,128)S(1)}, f32[96,1,384]{2,1,0:T(1,128)}, u32[]{:S(2)}) copy-start(f32[96,1,384]{2,1,0:T(1,128)} %get-tuple-element.155) | copy-start | bytes 442372
  1169.2 15.9 %copy-start.33 = (f32[192,768]{1,0:T(8,128)S(1)}, f32[192,768]{1,0:T(8,128)}, u32[]{:S(2)}) copy-start(f32[192,768]{1,0:T(8,128)} %get-tuple-element.159) | copy-start | bytes 1769476
  (46 other events, 149.3 us)
Sparse Core Ops, SparseCore 0:
  38.8 101.6 reduce-scatter.18
  248.2 34.0 reduce-scatter.24
  284.7 123.6 reduce-scatter.22
  410.7 123.8 reduce-scatter.20
  541.5 84.1 all-gather.6
  630.4 34.1 reduce-scatter.28
  721.5 33.4 reduce-scatter.26
  773.1 48.4 reduce-scatter.30
  902.5 59.7 all-gather.8
  971.1 54.9 all-reduce.8
  1028.7 33.0 reduce-scatter.32
